TPU v7x, 128 devices: a whole 4x4x4 slice. The times are simulated.
128 devices in a mesh: dp: 16 (over y_hi, z, core), fsdp: 8 (over x, y_lo).
Axes of the slice: x: 4, y: 4 (y_hi: 2, y_lo: 2; y = y_hi * 2 + y_lo), z: 4, core: 2. Of those that a mesh axis runs over, the one named last changes fastest.
Arguments:
- activations: bfloat16 [1, 16384, 8192], P(None, 'dp', 'fsdp'), may hold values from -6 to 6
- out_grads: bfloat16 [1, 16384, 22016], P(None, 'dp', 'fsdp'), may hold values from -2 to 2
- projector: bfloat16 [1, 8192, 1024], P(None, 'fsdp'), may hold values from -0.046875 to 0.046875
- first_moment: float32 [1, 22016, 1024], P(None, ('fsdp', 'dp')), may hold values from -16 to 16
- second_moment: float32 [1, 22016, 1024], P(None, ('fsdp', 'dp')), may hold values from 0.05 to 2
Outputs:
- weight_update: float32 [1, 8, 2752, 8192], P(None, None, 'dp', 'fsdp')
- first_new: float32 [1, 22016, 1024], P(None, ('fsdp', 'dp'))
- second_new: float32 [1, 22016, 1024], P(None, ('fsdp', 'dp'))
All inputs are finite; a program needn't handle non-finite values.
Results may differ from a plain program's by a relative error of at most 0.018.
Values may be sent and summed in bfloat16 or wider, within the bound.
A program may use at most 64 MiB of HBM per device.

v0:
```python
import jax
import jax.numpy as jnp
from jax import lax
from jax.sharding import PartitionSpec as P

beta_first = 0.9
beta_second = 0.999
adam_count = 100.0
epsilon = 1e-08


def adam_direction(grad_low, first, second):
    first_next = beta_first * first + (1.0 - beta_first) * grad_low
    second_next = beta_second * second + (1.0 - beta_second) * grad_low * grad_low
    bias_first = 1.0 - beta_first**adam_count
    bias_second = 1.0 - beta_second**adam_count
    direction = first_next / bias_first / (jnp.sqrt(second_next / bias_second) + epsilon)
    return (first_next, second_next, direction.astype(jnp.bfloat16))


def local(activations, out_grads, projector, first_moment, second_moment):
    owned_cols = first_moment.shape[1]
    fsdp_count = lax.axis_size("fsdp")
    features = activations[0]
    grads = out_grads[0]
    basis = projector[0]
    partial_value = jnp.dot(features, basis, preferred_element_type=jnp.float32)
    projected = lax.psum(partial_value.astype(jnp.bfloat16), "fsdp")
    grad_low = lax.psum_scatter(
        lax.dot_general(
            grads, projected, (((0,), (0,)), ((), ())), preferred_element_type=jnp.float32
        ).astype(jnp.bfloat16),
        "dp",
        scatter_dimension=0,
        tiled=True,
    ).astype(jnp.float32)
    first_next, second_next, direction = adam_direction(grad_low, first_moment[0], second_moment[0])
    expanded = lax.dot_general(
        lax.all_gather(direction, "fsdp", axis=0, tiled=True),
        basis,
        (((1,), (1,)), ((), ())),
        preferred_element_type=jnp.float32,
    )
    updates = [expanded.reshape(fsdp_count, owned_cols, basis.shape[0])]
    firsts = [first_next]
    seconds = [second_next]
    return (jnp.stack(updates), jnp.stack(firsts), jnp.stack(seconds))


def solution(mesh):
    in_specs = (
        P(None, "dp", "fsdp"),
        P(None, "dp", "fsdp"),
        P(None, "fsdp", None),
        P(None, ("fsdp", "dp"), None),
        P(None, ("fsdp", "dp"), None),
    )
    out_specs = (
        P(None, None, "dp", "fsdp"),
        P(None, ("fsdp", "dp"), None),
        P(None, ("fsdp", "dp"), None),
    )
    return jax.shard_map(local, mesh=mesh, in_specs=in_specs, out_specs=out_specs, check_vma=False)
```

profile of v0, /device:TPU:0, one launch (start us, length us, event | category | flops | bytes accessed | tf_op | source)
XLA Modules:
  0.0 279.7 jit_solution(18225023140092715757)
XLA Ops:
  7.2 0.0 copy-start
  7.2 0.0 all-reduce.4.cloned.1.call-start
  7.2 1.5 copy-done
  8.8 5.2 %fusion.9 = bf16[1024,1024]{1,0:T(8,128)(2,1)} fusion(bf16[1,1024,1024]{2,1,0:T(8,128)(2,1)S(1)} %copy-done, bf16[1,1024,1024]{2,1,0:T(8,128)(2,1)} %param.5), kind=kOutput, calls=%fused_computation.8 | convolution fusion | flops 2148532224 | bytes 6291456 | tf_op jit(solution)/shard_map/dot_general | solution.py:27
  14.0 0.0 all-reduce.4.cloned.1.call-update
  14.0 0.0 all-gather.3.cloned.1.call-start
  14.1 106.4 %all-reduce.4.cloned.1.call-done = bf16[1024,1024]{1,0:T(8,128)(2,1)} async-done(((bf16[1024,1024]{1,0:T(8,128)(2,1)}), bf16[1024,1024]{1,0:T(8,128)(2,1)}) %all-reduce.4.cloned.1.call-update) | async-done | bytes 2097168 | tf_op jit(solution)/shard_map/psum | solution.py:28
  120.5 10.2 %fusion.2 = bf16[2752,1024]{1,0:T(8,128)(2,1)} fusion(bf16[1024,1024]{1,0:T(8,128)(2,1)} %all-reduce.4.cloned.1.call-done, bf16[1,1024,2752]{1,2,0:T(8,128)(2,1)} %param.6), kind=kOutput, calls=%fused_computation.2 | convolution fusion | flops 5774180352 | bytes 13369344 | tf_op jit(solution)/shard_map/dot_general | solution.py:30
  130.7 0.0 copy-start.1
  130.7 53.5 %fusion = bf16[176,1024]{1,0:T(8,128)(2,1)S(1)} fusion(bf16[2752,1024]{1,0:T(8,128)(2,1)} %fusion.2), kind=kCustom, calls=%all-reduce-scatter | all-reduce-scatter fusion | flops 2883585 | bytes 5997056
  184.3 1.5 collective-permute-start
  185.8 0.0 copy-done.1
  185.8 0.6 dynamic-slice.4
  187.0 0.0 collective-permute-done
  187.0 3.4 %concatenate = bf16[236,1024]{1,0:T(8,128)(2,1)} concatenate(bf16[60,1024]{1,0:T(8,128)(2,1)S(1)} %collective-permute-done, bf16[176,1024]{1,0:T(8,128)(2,1)S(1)} %fusion), dimensions={0} | concatenate | bytes 966656
  190.5 2.8 fusion.17
  193.2 0.0 all-gather.3.cloned.1.call-update
  193.2 1.6 copy.17
  194.8 1.6 copy.16
  196.4 65.6 %all-gather.3.cloned.1.call-done = bf16[8,172,1024]{2,1,0:T(8,128)(2,1)} async-done(((bf16[1,172,1024]{2,1,0:T(8,128)(2,1)}), bf16[8,172,1024]{2,1,0:T(8,128)(2,1)}) %all-gather.3.cloned.1.call-update) | async-done | bytes 2818064 | tf_op jit(solution)/shard_map/all_gather | solution.py:39
  262.0 5.0 %convolution_bitcast_fusion = f32[1,8,172,1024]{3,2,1,0:T(8,128)S(1)} fusion(bf16[8,172,1024]{2,1,0:T(8,128)(2,1)} %all-gather.3.cloned.1.call-done, bf16[1,1024,1024]{2,1,0:T(8,128)(2,1)S(1)} %copy-done), kind=kOutput, calls=%fused_computation.3 | convolution fusion | flops 2885681152 | bytes 10551296 | tf_op jit(solution)/shard_map/dot_general | solution.py:38
  267.1 5.8 %copy.15 = f32[1,8,172,1024]{3,1,2,0:T(8,128)} copy(f32[1,8,172,1024]{3,2,1,0:T(8,128)S(1)} %convolution_bitcast_fusion) | data formatting | bytes 11272192
  (1 shorter events, 0.0 us)
Async XLA Ops:
  7.2 1.6 copy-start
  7.2 113.3 %all-reduce.4.cloned.1.call-start = ((), (), s32[]{:S(2)}) async-start(), calls=%async_computation | async-start | bytes 4194304 | tf_op jit(solution)/shard_map/psum | solution.py:28
  14.0 248.0 %all-gather.3.cloned.1.call-start = ((), (), s32[]{:S(2)}) async-start(), calls=%async_computation.1 | async-start | bytes 3244032 | tf_op jit(solution)/shard_map/all_gather | solution.py:39
  130.7 55.1 %copy-start.1 = (u32[128]{0:T(128)S(1)}, u32[128]{0:T(128)}, u32[]{:S(2)}) copy-start(u32[128]{0:T(128)} %constant.20) | copy-start | bytes 1540
  184.3 2.7 collective-permute-start
Sparse Core Ops, SparseCore 0:
  14.1 106.3 all-reduce.3
  193.4 68.5 all-gather.2
where the time goes:
time: 281 us; the launch traced here: 280 us
  waiting for transfers between devices  172 us (61%)
  blocking collectives  53.5 us (19%)
  matrix products  20.5 us (7%)
  between operations  14.8 us (5%)
  local copies, waits for them, and re-layouts  14.5 us (5%)
    psum x1, waiting for transfers between devices, local(): projected = lax.psum(partial_value.astype(jnp.bfloat16), 'fsdp')  106 us
    all_gather x1, waiting for transfers between devices, local(): lax.all_gather(direction, 'fsdp', axis=0, tiled=True)  65.6 us
    unnamed x1, blocking collectives  53.5 us
    unnamed x10, local copies, waits for them, and re-layouts  14.5 us
    dot_general x1, matrix products, local(): lax.dot_general(grads, projected, (((0,), (0,)), ((), ())), preferred_ele...  10.2 us
  transfers between devices with their start and end apart: 3, of which 2 were waited for; matrix products, arithmetic and copies ran while one was open for 1% of the time, Pallas kernels for 0%

commit v1 on v0

v1 whole, which is shorter than its diff:
```python
import functools

import jax
import jax.numpy as jnp
from jax import lax
from jax.experimental import pallas as pl
from jax.experimental.pallas import tpu as pltpu
from jax.sharding import PartitionSpec as P

MESH = pl.DeviceIdType.MESH
F32, BF16 = jnp.float32, jnp.bfloat16

beta_first = 0.9
beta_second = 0.999
adam_count = 100.0
epsilon = 1e-08

CHUNKS = 4
RS_X_FIRST = (True, False, True, False)
AG_X_FIRST = (False, True, False, True)
DIR_X_FIRST = (True, False, True, False)
STAGE_AT = (0, 6, 9, 11, 16, 20, 28, 31, 34, 39)
CHUNK_EVERY = 9.0


def adam_direction(grad_low, first, second):
    first_next = beta_first * first + (1.0 - beta_first) * grad_low
    second_next = beta_second * second + (1.0 - beta_second) * grad_low * grad_low
    bias_first = 1.0 - beta_first**adam_count
    bias_second = 1.0 - beta_second**adam_count
    direction = first_next / bias_first / (jnp.sqrt(second_next / bias_second) + epsilon)
    return (first_next, second_next, direction.astype(BF16))


def strips(rows, step, body):
    def one(index, carry):
        body(pl.ds(pl.multiple_of(index * step, step), step))
        return carry

    lax.fori_loop(0, rows // step, one, 0)


def wide(ref, *index):
    return ref[index].astype(F32)


def exchange_kernel(
    act_hbm, grads_hbm, basis_hbm, first_hbm, second_hbm,
    dirs_hbm, first_out, second_out,
    act, basis, grads_t, first, second, product,
    part, rs_a, rs_s, rs_b, projected,
    terms, core_in, z_out, z_in, y_out, y_in, dirs,
    load_sem, store_sem, send_sem, recv_sem,
):
    dp, fs = lax.axis_index("dp"), lax.axis_index("fsdp")
    yh, z, core = dp // 8, (dp // 2) % 4, dp % 2
    x, yl = fs // 2, fs % 2
    chunk = basis.shape[1] // CHUNKS
    row_tiles = basis.shape[1] // 128
    owned = first.shape[0] // row_tiles
    padded = dirs.shape[3]
    tokens = part.shape[3]
    features = act.shape[0]

    def along_x(d):
        return (dp, ((x + d) % 4) * 2 + yl)

    def along_z(d):
        return (yh * 8 + ((z + d) % 4) * 2 + core, fs)

    y_near = (dp, x * 2 + 1 - yl)
    y_far = ((1 - yh) * 8 + z * 2 + core, fs)
    sibling = (yh * 8 + z * 2 + 1 - core, fs)

    loads = [
        pltpu.make_async_copy(act_hbm.at[0], act, load_sem.at[0]),
        pltpu.make_async_copy(basis_hbm.at[0], basis, load_sem.at[1]),
        pltpu.make_async_copy(grads_hbm.at[0], grads_t, load_sem.at[2]),
        pltpu.make_async_copy(first_hbm, first, load_sem.at[3]),
        pltpu.make_async_copy(second_hbm, second, load_sem.at[4]),
    ]
    for load in loads:
        load.start()

    barrier = pltpu.get_barrier_semaphore()
    peers = [along_x(1), along_x(2), along_x(3), along_z(1), along_z(2), along_z(3), y_near, y_far, sibling]
    for peer in peers:
        pl.semaphore_signal(barrier, inc=1, device_id=peer, device_id_type=MESH)

    sent = []

    def remote(source, target, c, slot, peer):
        return pltpu.make_async_remote_copy(
            src_ref=source, dst_ref=target, send_sem=send_sem.at[c, slot], recv_sem=recv_sem.at[c, slot],
            device_id=peer, device_id_type=MESH,
        )

    def send(source, target, c, slot, peer):
        copy = remote(source, target, c, slot, peer)
        copy.start()
        sent.append(copy)

    def arrived(target, c, slot, peer):
        remote(target, target, c, slot, peer).wait_recv()


    def project(c):
        columns = slice(c * chunk, (c + 1) * chunk)
        half = features // 2

        def one(index, carry):
            rows = pl.ds(pl.multiple_of(index * half, half), half)
            value = jnp.dot(act[rows, :], basis[:, columns], preferred_element_type=F32)
            part[c, index] = value.astype(BF16).reshape(4, tokens, chunk)
            return carry

        lax.fori_loop(0, 2, one, 0)

    def reduce_first(c):
        if RS_X_FIRST[c]:
            for d in (2, 1, 3):
                send(part.at[c, :, (x + d) % 4], rs_a.at[c, pl.ds((d - 1) * 2, 2)], c, d - 1, along_x(d))
        else:
            send(part.at[c, 1 - yl], rs_a.at[c, pl.ds(0, 4)], c, 3, y_near)

    def reduce_second(c):
        if RS_X_FIRST[c]:
            for d in (1, 3, 2):
                arrived(rs_a.at[c, pl.ds((d - 1) * 2, 2)], c, d - 1, along_x(d))
            other = 1 - yl

            def body(rows):
                total = wide(part, c, other, x, rows)
                for d in range(3):
                    total += wide(rs_a, c, 2 * d + other, rows)
                rs_s[c, 0, rows] = total.astype(BF16)

            strips(tokens, 32, body)
            send(rs_s.at[c, 0], rs_b.at[c, 0], c, 3, y_near)
        else:
            arrived(rs_a.at[c, pl.ds(0, 4)], c, 3, y_near)
            for d in (2, 1, 3):
                to = (x + d) % 4

                def body(rows):
                    total = wide(part, c, yl, to, rows) + wide(rs_a, c, to, rows)
                    rs_s[c, d - 1, rows] = total.astype(BF16)

                strips(tokens, 32, body)
                send(rs_s.at[c, d - 1], rs_b.at[c, d - 1], c, d - 1, along_x(d))

    def reduce_last(c):
        if RS_X_FIRST[c]:
            arrived(rs_b.at[c, 0], c, 3, y_near)

            def body(rows):
                total = wide(part, c, yl, x, rows) + wide(rs_b, c, 0, rows)
                for d in range(3):
                    total += wide(rs_a, c, 2 * d + yl, rows)
                projected[c, yl, x, rows] = total.astype(BF16)

        else:
            for d in (1, 3, 2):
                arrived(rs_b.at[c, d - 1], c, d - 1, along_x(d))

            def body(rows):
                total = wide(part, c, yl, x, rows) + wide(rs_a, c, x, rows)
                for d in range(3):
                    total += wide(rs_b, c, d, rows)
                projected[c, yl, x, rows] = total.astype(BF16)

        strips(tokens, 32, body)

    def gather_first(buffer, c, slot, x_first):
        mine = buffer.at[c, yl, x]
        if x_first:
            for d in (2, 1, 3):
                send(mine, mine, c, slot + d - 1, along_x(d))
        else:
            send(mine, mine, c, slot + 3, y_near)

    def gather_second(buffer, c, slot, x_first):
        if x_first:
            for d in (1, 3, 2):
                arrived(buffer.at[c, yl, (x + 4 - d) % 4], c, slot + d - 1, along_x(d))
            send(buffer.at[c, yl], buffer.at[c, yl], c, slot + 3, y_near)
        else:
            arrived(buffer.at[c, 1 - yl, x], c, slot + 3, y_near)
            for d in (2, 1, 3):
                send(buffer.at[c, :, x], buffer.at[c, :, x], c, slot + d - 1, along_x(d))

    def gather_last(buffer, c, slot, x_first):
        if x_first:
            arrived(buffer.at[c, 1 - yl], c, slot + 3, y_near)
        else:
            for d in (1, 3, 2):
                arrived(buffer.at[c, :, (x + 4 - d) % 4], c, slot + d - 1, along_x(d))

    def gradient(c):
        rows_all = grads_t.shape[0]
        tile = rows_all // 4

        def one(index, carry):
            rows = pl.ds(pl.multiple_of(index * tile, tile), tile)
            value = jnp.dot(
                grads_t[rows, :], projected[c].reshape(features, chunk), preferred_element_type=F32
            )
            product[rows, :] = value
            return carry

        lax.fori_loop(0, 4, one, 0)

        def two(pair, carry):
            for which in range(2):
                shift = which * owned % 8
                start = pl.multiple_of(pair * (2 * owned) + which * owned - shift, 8)
                value = product[pl.ds(start, padded + 8), :]
                terms[c, which, pair // 4, pair % 4] = value[shift : shift + padded].astype(BF16)
            return carry

        lax.fori_loop(0, 8, two, 0)
        send(terms.at[c, 1 - core], core_in.at[c], c, 8, sibling)

    def core_sum(c):
        arrived(core_in.at[c], c, 8, sibling)
        for d in (2, 1, 3):
            to = (z + d) % 4
            for h in range(2):

                def body(rows):
                    total = wide(terms, c, core, h, to, rows) + wide(core_in, c, h, to, rows)
                    z_out[c, d - 1, h, rows] = total.astype(BF16)

                strips(padded, 16, body)
            send(z_out.at[c, d - 1], z_in.at[c, d - 1], c, 8 + d, along_z(d))

    def z_sum(c, h, rows):
        total = wide(terms, c, core, h, z, rows) + wide(core_in, c, h, z, rows)
        for d in range(3):
            total += wide(z_in, c, d, h, rows)
        return total

    def z_stage(c):
        for d in (1, 3, 2):
            arrived(z_in.at[c, d - 1], c, 8 + d, along_z(d))

        def body(rows):
            y_out[c, rows] = z_sum(c, 1 - yh, rows).astype(BF16)

        strips(padded, 16, body)
        send(y_out.at[c], y_in.at[c], c, 12, y_far)

    def adam(c):
        if c == 0:
            loads[3].wait()
            loads[4].wait()
        arrived(y_in.at[c], c, 12, y_far)

        def update(start, rows):
            low = z_sum(c, yh, pl.ds(start, rows)) + wide(y_in, c, pl.ds(start, rows))
            for part_of in range(chunk // 128):
                lanes = slice(part_of * 128, (part_of + 1) * 128)
                column = c * (chunk // 128) + part_of
                here = pl.ds(start * row_tiles + column, rows, stride=row_tiles)
                first_next, second_next, direction = adam_direction(low[:, lanes], first[here, :], second[here, :])
                first[here, :] = first_next
                second[here, :] = second_next
                dirs[c, yl, x, pl.ds(start, rows), lanes] = direction

        whole = owned // 16 * 16

        def one(index, carry):
            update(pl.multiple_of(index * 16, 16), 16)
            return carry

        lax.fori_loop(0, whole // 16, one, 0)
        if owned > whole:
            update(whole, owned - whole)

    def out_copies(c):
        columns = pl.ds(c * chunk, chunk)
        return [pltpu.make_async_copy(dirs.at[c], dirs_hbm.at[:, :, :, columns], store_sem.at[c])]

    barrier_done = []

    def stage(s, c):
        if s == 0:
            if c == 0:
                loads[0].wait()
                loads[1].wait()
            project(c)
            if not barrier_done:
                pl.semaphore_wait(barrier, len(peers))
                barrier_done.append(True)
            reduce_first(c)
        elif s == 1:
            reduce_second(c)
        elif s == 2:
            reduce_last(c)
            gather_first(projected, c, 4, AG_X_FIRST[c])
        elif s == 3:
            gather_second(projected, c, 4, AG_X_FIRST[c])
        elif s == 4:
            gather_last(projected, c, 4, AG_X_FIRST[c])
            if c == 0:
                loads[2].wait()
            gradient(c)
        elif s == 5:
            core_sum(c)
        elif s == 6:
            z_stage(c)
        elif s == 7:
            adam(c)
            gather_first(dirs, c, 13, DIR_X_FIRST[c])
        elif s == 8:
            gather_second(dirs, c, 13, DIR_X_FIRST[c])
        else:
            gather_last(dirs, c, 13, DIR_X_FIRST[c])
            for copy in out_copies(c):
                copy.start()

    order = sorted(
        ((STAGE_AT[s] + (CHUNK_EVERY * c if s else 0.0), c, s) for c in range(CHUNKS) for s in range(len(STAGE_AT)))
    )
    moments = [
        pltpu.make_async_copy(first, first_out, store_sem.at[CHUNKS]),
        pltpu.make_async_copy(second, second_out, store_sem.at[CHUNKS + 1]),
    ]
    for _, c, s in order:
        stage(s, c)
        if s == 7 and c == CHUNKS - 1:
            for copy in moments:
                copy.start()
    for copy in sent:
        copy.wait_send()
    for c in range(CHUNKS):
        for copy in out_copies(c):
            copy.wait()
    for copy in moments:
        copy.wait()


def exchange(activations, grads_t, projector, first, second, owned):
    features = activations.shape[1]
    width = grads_t.shape[1]
    depth, rank = projector.shape[1:]
    padded = -(-owned // 16) * 16
    chunk = rank // CHUNKS
    tokens = features // 8
    in_hbm = pl.BlockSpec(memory_space=pl.ANY)
    C = CHUNKS
    scratch = [
        pltpu.VMEM((features, depth), BF16),
        pltpu.VMEM((depth, rank), BF16),
        pltpu.VMEM((width, features), BF16),
        pltpu.VMEM(first.shape, F32),
        pltpu.VMEM(first.shape, F32),
        pltpu.VMEM((width + 16, chunk), F32),
        pltpu.VMEM((C, 2, 4, tokens, chunk), BF16),
        pltpu.VMEM((C, 6, tokens, chunk), BF16),
        pltpu.VMEM((C, 3, tokens, chunk), BF16),
        pltpu.VMEM((C, 3, tokens, chunk), BF16),
        pltpu.VMEM((C, 2, 4, tokens, chunk), BF16),
        pltpu.VMEM((C, 2, 2, 4, padded, chunk), BF16),
        pltpu.VMEM((C, 2, 4, padded, chunk), BF16),
        pltpu.VMEM((C, 3, 2, padded, chunk), BF16),
        pltpu.VMEM((C, 3, 2, padded, chunk), BF16),
        pltpu.VMEM((C, padded, chunk), BF16),
        pltpu.VMEM((C, padded, chunk), BF16),
        pltpu.VMEM((C, 2, 4, padded, chunk), BF16),
        pltpu.SemaphoreType.DMA((5,)),
        pltpu.SemaphoreType.DMA((C + 2,)),
        pltpu.SemaphoreType.DMA((C, 17)),
        pltpu.SemaphoreType.DMA((C, 17)),
    ]
    return pl.pallas_call(
        exchange_kernel,
        out_shape=(
            jax.ShapeDtypeStruct((2, 4, padded, rank), BF16),
            jax.ShapeDtypeStruct(first.shape, F32),
            jax.ShapeDtypeStruct(first.shape, F32),
        ),
        in_specs=[in_hbm] * 5,
        out_specs=(in_hbm,) * 3,
        scratch_shapes=scratch,
        compiler_params=pltpu.CompilerParams(
            collective_id=0, has_side_effects=True, vmem_limit_bytes=60 << 20
        ),
        name="exchange",
    )(activations, grads_t, projector, first, second)


def expand_kernel(
    dirs_hbm, basis, first_in, second_in, update_out, first_out, second_out, dirs, update, load_sem, store_sem, sem
):
    load = pltpu.make_async_copy(dirs_hbm, dirs, load_sem)
    load.start()
    moments = [
        pltpu.make_async_copy(first_in, first_out, sem.at[0]),
        pltpu.make_async_copy(second_in, second_out, sem.at[1]),
    ]
    for copy in moments:
        copy.start()
    padded, rank = dirs.shape[2:]
    owned = update.shape[1] // 8
    depth = basis.shape[1]
    load.wait()

    def store(column):
        return pltpu.make_async_copy(
            update.at[column], update_out.at[:, pl.ds(pl.multiple_of(column * 128, 128), 128)], store_sem.at[column]
        )

    def tile(index, carry):
        rows = pl.ds(pl.multiple_of(index * 256, 256), 256)
        total = lax.dot_general(
            dirs[...].reshape(8 * padded, rank), basis[0, rows, :],
            (((1,), (1,)), ((), ())), preferred_element_type=F32,
        )
        for half in range(2):
            for yl in range(2):
                for x in range(4):
                    start = (yl * 4 + x) * padded
                    update[index * 2 + half, pl.ds(x * 2 + yl, owned, stride=8), :] = total[
                        start : start + owned, half * 128 : (half + 1) * 128
                    ]
            store(index * 2 + half).start()
        return carry

    lax.fori_loop(0, depth // 256, tile, 0)
    for column in range(depth // 128):
        store(column).wait()
    for copy in moments:
        copy.wait()


def expand(dirs, projector, first, second, owned):
    depth, rank = projector.shape[1:]
    in_hbm = pl.BlockSpec(memory_space=pl.ANY)
    moment = jax.ShapeDtypeStruct(first.shape, F32)
    return pl.pallas_call(
        expand_kernel,
        out_shape=(jax.ShapeDtypeStruct((owned * 8, depth), F32), moment, moment),
        in_specs=[in_hbm, pl.BlockSpec(memory_space=pltpu.VMEM), in_hbm, in_hbm],
        out_specs=(in_hbm,) * 3,
        scratch_shapes=[
            pltpu.VMEM(dirs.shape, BF16),
            pltpu.VMEM((depth // 128, owned * 8, 128), F32),
            pltpu.SemaphoreType.DMA,
            pltpu.SemaphoreType.DMA((depth // 128,)),
            pltpu.SemaphoreType.DMA((2,)),
        ],
        compiler_params=pltpu.CompilerParams(vmem_limit_bytes=48 << 20),
        name="expand",
    )(dirs, projector, first, second)


def local(activations, out_grads, projector, first_moment, second_moment):
    owned, rank = first_moment.shape[1:]
    flat = (owned * (rank // 128), 128)
    dirs, first, second = exchange(
        activations, jnp.swapaxes(out_grads, 1, 2), projector, first_moment.reshape(flat), second_moment.reshape(flat),
        owned,
    )
    update, first, second = expand(dirs, projector, first, second, owned)
    update = update.reshape(owned, 8, -1).transpose(1, 0, 2)[None]
    return update, first.reshape(first_moment.shape), second.reshape(second_moment.shape)


def solution(mesh):
    in_specs = (
        P(None, "dp", "fsdp"),
        P(None, "dp", "fsdp"),
        P(None, "fsdp", None),
        P(None, ("fsdp", "dp"), None),
        P(None, ("fsdp", "dp"), None),
    )
    out_specs = (
        P(None, None, "dp", "fsdp"),
        P(None, ("fsdp", "dp"), None),
        P(None, ("fsdp", "dp"), None),
    )
    return jax.shard_map(local, mesh=mesh, in_specs=in_specs, out_specs=out_specs, check_vma=False)
```

time: 281 us -> 133 us (0.47)
  the two profiles are of different devices: /device:TPU:0 before, /device:TPU:32 now
where the time goes in v1:
time: 133 us
  Pallas kernels  130 us (98%)
  local copies, waits for them, and re-layouts  2.21 us (2%)
    pallas_call x1, Pallas kernels, exchange(): pl.pallas_call(exchange_kernel, out_shape=(jax.ShapeDtypeStruct((2, 4, pa...  122 us
    pallas_call x1, Pallas kernels, expand(): pl.pallas_call(expand_kernel, out_shape=(jax.ShapeDtypeStruct((owned * 8,...  7.79 us

profile of v1, /device:TPU:32, one launch (start us, length us, event | category | flops | bytes accessed | tf_op | source)
XLA Modules:
  0.0 133.1 jit_solution(17687008900337991977)
XLA Ops:
  0.6 0.0 copy-start
  0.6 122.4 %exchange.1 = (bf16[2,4,176,1024]{3,2,1,0:T(8,128)(2,1)}, f32[1376,128]{1,0:T(8,128)}, f32[1376,128]{1,0:T(8,128)}) custom-call(bf16[1,1024,1024]{2,1,0:T(8,128)(2,1)} %act_hbm.1, bf16[1,2752,1024]{2,1,0:T(8,128)(2,1)} %bitcast.10, bf16[1,1024,1024]{2,1,0:T(8,128)(2,1)} %basis.1, f32[1376,128]{1,0:T(8,128)} %bitcast.11, f32[1376,128]{1,0:T(8,128)} %bitcast.12), custom_call_target="tpu_custom_call" | custom-call | tf_op jit(solution)/shard_map/exchange/pallas_call | solution.py:376
  123.0 0.0 copy-done
  123.1 0.0 copy-start.1
  123.1 1.1 copy-done.1
  124.2 0.0 copy-start.2
  124.2 1.1 copy-done.2
  125.3 7.8 %expand.1 = (f32[1376,1024]{1,0:T(8,128)}, f32[1376,128]{1,0:T(8,128)}, f32[1376,128]{1,0:T(8,128)}) custom-call(bf16[2,4,176,1024]{3,2,1,0:T(8,128)(2,1)} %get-tuple-element.9.dirs_hbm, bf16[1,1024,1024]{2,1,0:T(8,128)(2,1)S(1)} %copy-done, f32[1376,128]{1,0:T(8,128)S(1)} %copy-done.1, f32[1376,128]{1,0:T(8,128)S(1)} %copy-done.2), custom_call_target="tpu_custom_call" | custom-call | tf_op jit(solution)/shard_map/expand/pallas_call | solution.py:441
Async XLA Ops:
  0.6 122.4 %copy-start = (bf16[1,1024,1024]{2,1,0:T(8,128)(2,1)S(1)}, bf16[1,1024,1024]{2,1,0:T(8,128)(2,1)}, u32[]{:S(2)}) copy-start(bf16[1,1024,1024]{2,1,0:T(8,128)(2,1)} %basis.1) | copy-start | bytes 6291460
  123.1 1.1 copy-start.1
  124.2 1.1 copy-start.2

commit v2 on v1

--- a/solution.py
+++ b/solution.py
@@ -15,12 +15,16 @@
 adam_count = 100.0
 epsilon = 1e-08
 
-CHUNKS = 4
-RS_X_FIRST = (True, False, True, False)
-AG_X_FIRST = (False, True, False, True)
-DIR_X_FIRST = (True, False, True, False)
-STAGE_AT = (0, 6, 9, 11, 16, 20, 28, 31, 34, 39)
-CHUNK_EVERY = 9.0
+CHUNKS = 8
+RS_X_FIRST = (True, False, True, False, True, False, True, False)
+AG_X_FIRST = (False, True, False, True, False, True, False, True)
+DIR_X_FIRST = (True, False, True, False, True, False, True, False)
+ORDER = (
+    4, 7, 3, 0, 7, 4, 5, 2, 4, 3, 7, 0, 1, 4, 0, 3, 2, 1, 7, 0,
+    6, 4, 3, 4, 2, 7, 5, 1, 7, 3, 2, 6, 0, 3, 4, 6, 1, 5, 0, 2,
+    6, 7, 5, 2, 1, 4, 3, 0, 7, 1, 6, 3, 5, 4, 0, 6, 7, 5, 3, 1,
+    2, 0, 7, 6, 5, 2, 1, 6, 5, 1, 2, 3, 5, 6, 1, 5, 4, 2, 0, 6,
+)
 
 
 def adam_direction(grad_low, first, second):
@@ -30,14 +34,6 @@
     bias_second = 1.0 - beta_second**adam_count
     direction = first_next / bias_first / (jnp.sqrt(second_next / bias_second) + epsilon)
     return (first_next, second_next, direction.astype(BF16))
-
-
-def strips(rows, step, body):
-    def one(index, carry):
-        body(pl.ds(pl.multiple_of(index * step, step), step))
-        return carry
-
-    lax.fori_loop(0, rows // step, one, 0)
 
 
 def wide(ref, *index):
@@ -105,13 +101,15 @@
 
 
     def project(c):
-        columns = slice(c * chunk, (c + 1) * chunk)
+        columns = slice(c * chunk, (c + 2) * chunk)
         half = features // 2
 
         def one(index, carry):
             rows = pl.ds(pl.multiple_of(index * half, half), half)
             value = jnp.dot(act[rows, :], basis[:, columns], preferred_element_type=F32)
-            part[c, index] = value.astype(BF16).reshape(4, tokens, chunk)
+            value = value.astype(BF16)
+            for which in range(2):
+                part[c + which, index] = value[:, which * chunk : (which + 1) * chunk].reshape(4, tokens, chunk)
             return carry
 
         lax.fori_loop(0, 2, one, 0)
@@ -129,47 +127,31 @@
                 arrived(rs_a.at[c, pl.ds((d - 1) * 2, 2)], c, d - 1, along_x(d))
             other = 1 - yl
 
-            def body(rows):
-                total = wide(part, c, other, x, rows)
-                for d in range(3):
-                    total += wide(rs_a, c, 2 * d + other, rows)
-                rs_s[c, 0, rows] = total.astype(BF16)
-
-            strips(tokens, 32, body)
+            total = wide(part, c, other, x)
+            for d in range(3):
+                total += wide(rs_a, c, 2 * d + other)
+            rs_s[c, 0] = total.astype(BF16)
             send(rs_s.at[c, 0], rs_b.at[c, 0], c, 3, y_near)
         else:
             arrived(rs_a.at[c, pl.ds(0, 4)], c, 3, y_near)
             for d in (2, 1, 3):
                 to = (x + d) % 4
-
-                def body(rows):
-                    total = wide(part, c, yl, to, rows) + wide(rs_a, c, to, rows)
-                    rs_s[c, d - 1, rows] = total.astype(BF16)
-
-                strips(tokens, 32, body)
+                rs_s[c, d - 1] = (wide(part, c, yl, to) + wide(rs_a, c, to)).astype(BF16)
                 send(rs_s.at[c, d - 1], rs_b.at[c, d - 1], c, d - 1, along_x(d))
 
     def reduce_last(c):
         if RS_X_FIRST[c]:
             arrived(rs_b.at[c, 0], c, 3, y_near)
-
-            def body(rows):
-                total = wide(part, c, yl, x, rows) + wide(rs_b, c, 0, rows)
-                for d in range(3):
-                    total += wide(rs_a, c, 2 * d + yl, rows)
-                projected[c, yl, x, rows] = total.astype(BF16)
-
+            total = wide(part, c, yl, x) + wide(rs_b, c, 0)
+            for d in range(3):
+                total += wide(rs_a, c, 2 * d + yl)
         else:
             for d in (1, 3, 2):
                 arrived(rs_b.at[c, d - 1], c, d - 1, along_x(d))
-
-            def body(rows):
-                total = wide(part, c, yl, x, rows) + wide(rs_a, c, x, rows)
-                for d in range(3):
-                    total += wide(rs_b, c, d, rows)
-                projected[c, yl, x, rows] = total.astype(BF16)
-
-        strips(tokens, 32, body)
+            total = wide(part, c, yl, x) + wide(rs_a, c, x)
+            for d in range(3):
+                total += wide(rs_b, c, d)
+        projected[c, yl, x] = total.astype(BF16)
 
     def gather_first(buffer, c, slot, x_first):
         mine = buffer.at[c, yl, x]
@@ -226,69 +208,51 @@
         for d in (2, 1, 3):
             to = (z + d) % 4
             for h in range(2):
-
-                def body(rows):
-                    total = wide(terms, c, core, h, to, rows) + wide(core_in, c, h, to, rows)
-                    z_out[c, d - 1, h, rows] = total.astype(BF16)
-
-                strips(padded, 16, body)
+                z_out[c, d - 1, h] = (wide(terms, c, core, h, to) + wide(core_in, c, h, to)).astype(BF16)
             send(z_out.at[c, d - 1], z_in.at[c, d - 1], c, 8 + d, along_z(d))
 
-    def z_sum(c, h, rows):
-        total = wide(terms, c, core, h, z, rows) + wide(core_in, c, h, z, rows)
+    def z_sum(c, h):
+        total = wide(terms, c, core, h, z) + wide(core_in, c, h, z)
         for d in range(3):
-            total += wide(z_in, c, d, h, rows)
+            total += wide(z_in, c, d, h)
         return total
 
     def z_stage(c):
         for d in (1, 3, 2):
             arrived(z_in.at[c, d - 1], c, 8 + d, along_z(d))
-
-        def body(rows):
-            y_out[c, rows] = z_sum(c, 1 - yh, rows).astype(BF16)
-
-        strips(padded, 16, body)
+        y_out[c] = z_sum(c, 1 - yh).astype(BF16)
         send(y_out.at[c], y_in.at[c], c, 12, y_far)
 
     def adam(c):
-        if c == 0:
+        if 3 not in waited:
             loads[3].wait()
             loads[4].wait()
+            waited.add(3)
         arrived(y_in.at[c], c, 12, y_far)
 
-        def update(start, rows):
-            low = z_sum(c, yh, pl.ds(start, rows)) + wide(y_in, c, pl.ds(start, rows))
-            for part_of in range(chunk // 128):
-                lanes = slice(part_of * 128, (part_of + 1) * 128)
-                column = c * (chunk // 128) + part_of
-                here = pl.ds(start * row_tiles + column, rows, stride=row_tiles)
-                first_next, second_next, direction = adam_direction(low[:, lanes], first[here, :], second[here, :])
-                first[here, :] = first_next
-                second[here, :] = second_next
-                dirs[c, yl, x, pl.ds(start, rows), lanes] = direction
-
-        whole = owned // 16 * 16
-
-        def one(index, carry):
-            update(pl.multiple_of(index * 16, 16), 16)
-            return carry
-
-        lax.fori_loop(0, whole // 16, one, 0)
-        if owned > whole:
-            update(whole, owned - whole)
+        low = (z_sum(c, yh) + wide(y_in, c))[:owned]
+        for part_of in range(chunk // 128):
+            lanes = slice(part_of * 128, (part_of + 1) * 128)
+            here = pl.ds(c * (chunk // 128) + part_of, owned, stride=row_tiles)
+            first_next, second_next, direction = adam_direction(low[:, lanes], first[here, :], second[here, :])
+            first[here, :] = first_next
+            second[here, :] = second_next
+            dirs[c, yl, x, :owned, lanes] = direction
 
     def out_copies(c):
         columns = pl.ds(c * chunk, chunk)
         return [pltpu.make_async_copy(dirs.at[c], dirs_hbm.at[:, :, :, columns], store_sem.at[c])]
 
-    barrier_done = []
+    barrier_done, projected_pairs, waited = [], set(), set()
 
     def stage(s, c):
         if s == 0:
-            if c == 0:
+            if not projected_pairs:
                 loads[0].wait()
                 loads[1].wait()
-            project(c)
+            if c // 2 not in projected_pairs:
+                project(c // 2 * 2)
+                projected_pairs.add(c // 2)
             if not barrier_done:
                 pl.semaphore_wait(barrier, len(peers))
                 barrier_done.append(True)
@@ -302,8 +266,9 @@
             gather_second(projected, c, 4, AG_X_FIRST[c])
         elif s == 4:
             gather_last(projected, c, 4, AG_X_FIRST[c])
-            if c == 0:
+            if 2 not in waited:
                 loads[2].wait()
+                waited.add(2)
             gradient(c)
         elif s == 5:
             core_sum(c)
@@ -319,16 +284,18 @@
             for copy in out_copies(c):
                 copy.start()
 
-    order = sorted(
-        ((STAGE_AT[s] + (CHUNK_EVERY * c if s else 0.0), c, s) for c in range(CHUNKS) for s in range(len(STAGE_AT)))
-    )
+    order, turns = [], [0] * CHUNKS
+    for c in ORDER:
+        order.append((None, c, turns[c]))
+        turns[c] += 1
     moments = [
         pltpu.make_async_copy(first, first_out, store_sem.at[CHUNKS]),
         pltpu.make_async_copy(second, second_out, store_sem.at[CHUNKS + 1]),
     ]
+    last_adam = [c for _, c, s in order if s == 7][-1]
     for _, c, s in order:
         stage(s, c)
-        if s == 7 and c == CHUNKS - 1:
+        if s == 7 and c == last_adam:
             for copy in moments:
                 copy.start()
     for copy in sent:
@@ -390,48 +357,69 @@
     )(activations, grads_t, projector, first, second)
 
 
+EXPAND_ROWS = ((0, 64), (64, 64), (128, 48))
+
+
 def expand_kernel(
-    dirs_hbm, basis, first_in, second_in, update_out, first_out, second_out, dirs, update, load_sem, store_sem, sem
+    dirs_hbm, basis_hbm, first_in, second_in, update_out, first_out, second_out,
+    dirs, basis, update, first, second, load_sem, store_sem, sem,
 ):
-    load = pltpu.make_async_copy(dirs_hbm, dirs, load_sem)
-    load.start()
-    moments = [
-        pltpu.make_async_copy(first_in, first_out, sem.at[0]),
-        pltpu.make_async_copy(second_in, second_out, sem.at[1]),
-    ]
-    for copy in moments:
+    basis_load = pltpu.make_async_copy(basis_hbm.at[0], basis, sem.at[0])
+    basis_load.start()
+    loads = [
+        pltpu.make_async_copy(dirs_hbm.at[:, :, pl.ds(*rows)], dirs.at[:, :, pl.ds(*rows)], load_sem.at[group])
+        for group, rows in enumerate(EXPAND_ROWS)
+    ]
+    for load in loads:
+        load.start()
+    moments_in = [
+        pltpu.make_async_copy(first_in, first, sem.at[1]),
+        pltpu.make_async_copy(second_in, second, sem.at[2]),
+    ]
+    moments_out = [
+        pltpu.make_async_copy(first, first_out, sem.at[3]),
+        pltpu.make_async_copy(second, second_out, sem.at[4]),
+    ]
+    for copy in moments_in:
         copy.start()
-    padded, rank = dirs.shape[2:]
+    rank = dirs.shape[3]
+    depth = basis.shape[0]
     owned = update.shape[1] // 8
-    depth = basis.shape[1]
-    load.wait()
-
-    def store(column):
-        return pltpu.make_async_copy(
-            update.at[column], update_out.at[:, pl.ds(pl.multiple_of(column * 128, 128), 128)], store_sem.at[column]
-        )
-
-    def tile(index, carry):
-        rows = pl.ds(pl.multiple_of(index * 256, 256), 256)
-        total = lax.dot_general(
-            dirs[...].reshape(8 * padded, rank), basis[0, rows, :],
-            (((1,), (1,)), ((), ())), preferred_element_type=F32,
-        )
-        for half in range(2):
-            for yl in range(2):
-                for x in range(4):
-                    start = (yl * 4 + x) * padded
-                    update[index * 2 + half, pl.ds(x * 2 + yl, owned, stride=8), :] = total[
-                        start : start + owned, half * 128 : (half + 1) * 128
-                    ]
-            store(index * 2 + half).start()
-        return carry
-
-    lax.fori_loop(0, depth // 256, tile, 0)
-    for column in range(depth // 128):
-        store(column).wait()
-    for copy in moments:
-        copy.wait()
+    stores = []
+    basis_load.wait()
+    for group, (start, rows) in enumerate(EXPAND_ROWS):
+        loads[group].wait()
+        kept = min(rows, owned - start)
+
+        def tile(index, carry):
+            lanes = pl.ds(pl.multiple_of(index * 256, 256), 256)
+            total = lax.dot_general(
+                dirs[:, :, pl.ds(start, rows), :].reshape(8 * rows, rank), basis[lanes, :],
+                (((1,), (1,)), ((), ())), preferred_element_type=F32,
+            )
+            for half in range(2):
+                for yl in range(2):
+                    for x in range(4):
+                        at = (yl * 4 + x) * rows
+                        update[index * 2 + half, pl.ds(start * 8 + x * 2 + yl, kept, stride=8), :] = total[
+                            at : at + kept, half * 128 : (half + 1) * 128
+                        ]
+            return carry
+
+        lax.fori_loop(0, depth // 256, tile, 0)
+        for column in range(depth // 128):
+            place = pl.ds(start * 8, kept * 8)
+            store = pltpu.make_async_copy(
+                update.at[column, place], update_out.at[place, pl.ds(column * 128, 128)], store_sem.at[group, column]
+            )
+            store.start()
+            stores.append(store)
+        if group == 0:
+            for copy_in, copy_out in zip(moments_in, moments_out):
+                copy_in.wait()
+                copy_out.start()
+    for store in stores + moments_out:
+        store.wait()
 
 
 def expand(dirs, projector, first, second, owned):
@@ -441,16 +429,19 @@
     return pl.pallas_call(
         expand_kernel,
         out_shape=(jax.ShapeDtypeStruct((owned * 8, depth), F32), moment, moment),
-        in_specs=[in_hbm, pl.BlockSpec(memory_space=pltpu.VMEM), in_hbm, in_hbm],
+        in_specs=[in_hbm] * 4,
         out_specs=(in_hbm,) * 3,
         scratch_shapes=[
             pltpu.VMEM(dirs.shape, BF16),
+            pltpu.VMEM((depth, rank), BF16),
             pltpu.VMEM((depth // 128, owned * 8, 128), F32),
-            pltpu.SemaphoreType.DMA,
-            pltpu.SemaphoreType.DMA((depth // 128,)),
-            pltpu.SemaphoreType.DMA((2,)),
+            pltpu.VMEM(first.shape, F32),
+            pltpu.VMEM(first.shape, F32),
+            pltpu.SemaphoreType.DMA((len(EXPAND_ROWS),)),
+            pltpu.SemaphoreType.DMA((len(EXPAND_ROWS), depth // 128)),
+            pltpu.SemaphoreType.DMA((5,)),
         ],
-        compiler_params=pltpu.CompilerParams(vmem_limit_bytes=48 << 20),
+        compiler_params=pltpu.CompilerParams(vmem_limit_bytes=60 << 20),
         name="expand",
     )(dirs, projector, first, second)
 

time: 133 us -> 92.8 us (0.70)
  the two profiles are of different devices: /device:TPU:32 before, /device:TPU:0 now
where the time goes in v2:
time: 92.8 us; the launch traced here: 92.7 us
  Pallas kernels  92.1 us (99%)
    pallas_call x1, Pallas kernels, exchange(): pl.pallas_call(exchange_kernel, out_shape=(jax.ShapeDtypeStruct((2, 4, pa...  83.1 us
    pallas_call x1, Pallas kernels, expand(): pl.pallas_call(expand_kernel, out_shape=(jax.ShapeDtypeStruct((owned * 8,...  9.03 us

profile of v2, /device:TPU:0, one launch (start us, length us, event | category | flops | bytes accessed | tf_op | source)
XLA Modules:
  0.0 92.7 jit_solution(5846327452271320418)
XLA Ops:
  0.6 83.1 %exchange.1 = (bf16[2,4,176,1024]{3,2,1,0:T(8,128)(2,1)}, f32[1376,128]{1,0:T(8,128)}, f32[1376,128]{1,0:T(8,128)}) custom-call(bf16[1,1024,1024]{2,1,0:T(8,128)(2,1)} %act_hbm.1, bf16[1,2752,1024]{2,1,0:T(8,128)(2,1)} %bitcast.10, bf16[1,1024,1024]{2,1,0:T(8,128)(2,1)} %basis_hbm.3, f32[1376,128]{1,0:T(8,128)} %bitcast.11, f32[1376,128]{1,0:T(8,128)} %bitcast.12), custom_call_target="tpu_custom_call" | custom-call | tf_op jit(solution)/shard_map/exchange/pallas_call | solution.py:343
  83.7 9.0 %expand.1 = (f32[1376,1024]{1,0:T(8,128)}, f32[1376,128]{1,0:T(8,128)}, f32[1376,128]{1,0:T(8,128)}) custom-call(bf16[2,4,176,1024]{3,2,1,0:T(8,128)(2,1)} %get-tuple-element.9.dirs_hbm, bf16[1,1024,1024]{2,1,0:T(8,128)(2,1)} %basis_hbm.3, f32[1376,128]{1,0:T(8,128)} %get-tuple-element.10.first_in, f32[1376,128]{1,0:T(8,128)} %get-tuple-element.11.second_in), custom_call_target="tpu_custom_call" | custom-call | tf_op jit(solution)/shard_map/expand/pallas_call | solution.py:429

commit v3 on v2

v3 whole, which is shorter than its diff:
```python
import functools

import jax
import jax.numpy as jnp
from jax import lax
from jax.experimental import pallas as pl
from jax.experimental.pallas import tpu as pltpu
from jax.sharding import PartitionSpec as P

MESH = pl.DeviceIdType.MESH
F32, BF16 = jnp.float32, jnp.bfloat16

beta_first = 0.9
beta_second = 0.999
adam_count = 100.0
epsilon = 1e-08

CHUNKS = 8
RS_X_FIRST = (True, False, True, False, True, False, True, False)
AG_X_FIRST = (True, False, True, False, True, False, True, False)
DIR_X_FIRST = (True, False, True, False, True, False, True, False)
ORDER = (
    2, 3, 7, 0, 3, 6, 2, 1, 2, 3, 0, 7, 6, 3, 2, 1, 6, 0, 7, 5,
    2, 3, 6, 7, 4, 0, 2, 5, 3, 1, 7, 6, 4, 1, 2, 5, 7, 0, 3, 4,
    6, 1, 7, 5, 4, 2, 0, 6, 1, 7, 3, 2, 4, 5, 6, 3, 0, 7, 4, 1,
    2, 5, 6, 4, 3, 0, 1, 6, 7, 5, 0, 4, 1, 5, 4, 0, 1, 5, 4, 5,
)


def adam_direction(grad_low, first, second):
    first_next = beta_first * first + (1.0 - beta_first) * grad_low
    second_next = beta_second * second + (1.0 - beta_second) * grad_low * grad_low
    bias_first = 1.0 - beta_first**adam_count
    bias_second = 1.0 - beta_second**adam_count
    direction = first_next / bias_first / (jnp.sqrt(second_next / bias_second) + epsilon)
    return (first_next, second_next, direction.astype(BF16))


def wide(ref, *index):
    return ref[index].astype(F32)


def exchange_kernel(
    act_hbm, grads_hbm, basis_hbm, first_hbm, second_hbm,
    dirs_hbm, first_out, second_out,
    act, basis, grads_t, first, second, product,
    part, rs_a, rs_s, rs_b, projected,
    terms, core_in, z_out, z_in, y_out, y_in, dirs,
    load_sem, store_sem, send_sem, recv_sem,
):
    dp, fs = lax.axis_index("dp"), lax.axis_index("fsdp")
    yh, z, core = dp // 8, (dp // 2) % 4, dp % 2
    x, yl = fs // 2, fs % 2
    chunk = basis.shape[1] // CHUNKS
    row_tiles = basis.shape[1] // 128
    owned = first.shape[0] // row_tiles
    padded = dirs.shape[3]
    tokens = part.shape[3]
    features = act.shape[0]

    to_x = [None] + [(x + d) % 4 for d in (1, 2, 3)]
    to_z = [None] + [(z + d) % 4 for d in (1, 2, 3)]
    x_peers = [None] + [(dp, to_x[d] * 2 + yl) for d in (1, 2, 3)]
    z_peers = [None] + [(yh * 8 + to_z[d] * 2 + core, fs) for d in (1, 2, 3)]
    y_near = (dp, x * 2 + 1 - yl)
    y_far = ((1 - yh) * 8 + z * 2 + core, fs)
    sibling = (yh * 8 + z * 2 + 1 - core, fs)

    half = features // 2
    pair = 2 * chunk
    act_loads = [
        pltpu.make_async_copy(act_hbm.at[0, pl.ds(i * half, half)], act.at[pl.ds(i * half, half)], load_sem.at[i])
        for i in range(2)
    ]
    basis_loads = [
        pltpu.make_async_copy(
            basis_hbm.at[0, :, pl.ds(i * pair, pair)], basis.at[:, pl.ds(i * pair, pair)], load_sem.at[2 + i]
        )
        for i in range(CHUNKS // 2)
    ]
    grads_load = pltpu.make_async_copy(grads_hbm.at[0], grads_t, load_sem.at[2 + CHUNKS // 2])
    moment_loads = [
        pltpu.make_async_copy(first_hbm, first, load_sem.at[3 + CHUNKS // 2]),
        pltpu.make_async_copy(second_hbm, second, load_sem.at[4 + CHUNKS // 2]),
    ]
    pairs = list(dict.fromkeys(c // 2 for c in ORDER))
    basis_loads[pairs[0]].start()
    for load in act_loads + [basis_loads[i] for i in pairs[1:]] + [grads_load] + moment_loads:
        load.start()

    barrier = pltpu.get_barrier_semaphore()
    peers = x_peers[1:] + z_peers[1:] + [y_near, y_far, sibling]
    for peer in peers:
        pl.semaphore_signal(barrier, inc=1, device_id=peer, device_id_type=MESH)

    sent = [[] for _ in range(CHUNKS)]

    def remote(source, target, c, slot, peer):
        return pltpu.make_async_remote_copy(
            src_ref=source, dst_ref=target, send_sem=send_sem.at[c, slot], recv_sem=recv_sem.at[c, slot],
            device_id=peer, device_id_type=MESH,
        )

    def send(source, target, c, slot, peer):
        copy = remote(source, target, c, slot, peer)
        copy.start()
        sent[c].append(copy)

    def arrived(target, c, slot, peer):
        remote(target, target, c, slot, peer).wait_recv()


    def project(c):
        basis_loads[c // 2].wait()
        for index in range(2):
            if "act" not in waited:
                act_loads[index].wait()
            value = jnp.dot(
                act[index * half : (index + 1) * half, :], basis[:, c * chunk : (c + 2) * chunk],
                preferred_element_type=F32,
            ).astype(BF16)
            for which in range(2):
                part[c + which, index] = value[:, which * chunk : (which + 1) * chunk].reshape(4, tokens, chunk)
        waited.add("act")

    def reduce_first(c):
        if RS_X_FIRST[c]:
            for d in (2, 1, 3):
                send(part.at[c, :, to_x[d]], rs_a.at[c, pl.ds((d - 1) * 2, 2)], c, d - 1, x_peers[d])
        else:
            send(part.at[c, 1 - yl], rs_a.at[c, pl.ds(0, 4)], c, 3, y_near)

    def reduce_second(c):
        if RS_X_FIRST[c]:
            for d in (1, 3, 2):
                arrived(rs_a.at[c, pl.ds((d - 1) * 2, 2)], c, d - 1, x_peers[d])
            other = 1 - yl

            total = wide(part, c, other, x)
            for d in range(3):
                total += wide(rs_a, c, 2 * d + other)
            rs_s[c, 0] = total.astype(BF16)
            send(rs_s.at[c, 0], rs_b.at[c, 0], c, 3, y_near)
        else:
            arrived(rs_a.at[c, pl.ds(0, 4)], c, 3, y_near)
            for d in (2, 1, 3):
                to = to_x[d]
                rs_s[c, d - 1] = (wide(part, c, yl, to) + wide(rs_a, c, to)).astype(BF16)
                send(rs_s.at[c, d - 1], rs_b.at[c, d - 1], c, d - 1, x_peers[d])

    def reduce_last(c):
        if RS_X_FIRST[c]:
            arrived(rs_b.at[c, 0], c, 3, y_near)
            total = wide(part, c, yl, x) + wide(rs_b, c, 0)
            for d in range(3):
                total += wide(rs_a, c, 2 * d + yl)
        else:
            for d in (1, 3, 2):
                arrived(rs_b.at[c, d - 1], c, d - 1, x_peers[d])
            total = wide(part, c, yl, x) + wide(rs_a, c, x)
            for d in range(3):
                total += wide(rs_b, c, d)
        projected[c, yl, x] = total.astype(BF16)

    def gather_first(buffer, target, c, slot, x_first):
        mine, there = buffer.at[c, yl, x], target.at[yl, x]
        send(mine, there if x_first else mine, c, slot + 3, y_near)
        for d in (2, 1, 3):
            send(mine, mine if x_first else there, c, slot + d - 1, x_peers[d])

    def gather_second(buffer, target, c, slot, x_first):
        if x_first:
            for d in (1, 3, 2):
                block = (yl, to_x[4 - d])
                arrived(buffer.at[(c,) + block], c, slot + d - 1, x_peers[d])
                send(buffer.at[(c,) + block], target.at[block], c, slot + 3 + d, y_near)
        else:
            block = (1 - yl, x)
            arrived(buffer.at[(c,) + block], c, slot + 3, y_near)
            for d in (2, 1, 3):
                send(buffer.at[(c,) + block], target.at[block], c, slot + 3 + d, x_peers[d])

    def gather_last(target, c, slot, x_first):
        if x_first:
            arrived(target.at[1 - yl, x], c, slot + 3, y_near)
            for d in (1, 3, 2):
                arrived(target.at[1 - yl, to_x[4 - d]], c, slot + 3 + d, y_near)
        else:
            for d in (1, 3, 2):
                arrived(target.at[yl, to_x[4 - d]], c, slot + d - 1, x_peers[d])
            for d in (1, 3, 2):
                arrived(target.at[1 - yl, to_x[4 - d]], c, slot + 3 + d, x_peers[d])

    def gradient(first_c):
        rows_all = grads_t.shape[0]
        tile = rows_all // 4

        def one(index, carry):
            rows = pl.ds(pl.multiple_of(index * tile, tile), tile)
            right = jnp.concatenate([projected[first_c + k].reshape(features, chunk) for k in range(2)], axis=1)
            product[rows, :] = jnp.dot(grads_t[rows, :], right, preferred_element_type=F32)
            return carry

        lax.fori_loop(0, 4, one, 0)

        def two(pair, carry):
            for which in range(2):
                shift = which * owned % 8
                start = pl.multiple_of(pair * (2 * owned) + which * owned - shift, 8)
                value = product[pl.ds(start, padded + 8), :]
                value = value[shift : shift + padded].astype(BF16)
                for k in range(2):
                    terms[first_c + k, which, pair // 4, pair % 4] = value[:, k * chunk : (k + 1) * chunk]
            return carry

        lax.fori_loop(0, 8, two, 0)
        for c in (first_c, first_c + 1):
            send(terms.at[c, 1 - core], core_in.at[c], c, 11, sibling)

    def core_sum(c):
        arrived(core_in.at[c], c, 11, sibling)
        for h, slot in ((1 - yh, 11), (yh, 14)):
            for d in (2, 1, 3):
                to = to_z[d]
                z_out[c, d - 1, h] = (wide(terms, c, core, h, to) + wide(core_in, c, h, to)).astype(BF16)
                send(z_out.at[c, d - 1, h], z_in.at[c, d - 1, h], c, slot + d, z_peers[d])

    def z_arrived(c, h, slot):
        for d in (1, 3, 2):
            arrived(z_in.at[c, d - 1, h], c, slot + d, z_peers[d])

    def z_sum(c, h):
        total = wide(terms, c, core, h, z) + wide(core_in, c, h, z)
        for d in range(3):
            total += wide(z_in, c, d, h)
        return total

    def z_stage(c):
        z_arrived(c, 1 - yh, 11)
        y_out[c] = z_sum(c, 1 - yh).astype(BF16)
        send(y_out.at[c], y_in.at[c], c, 18, y_far)

    def adam(c):
        if "moments" not in waited:
            for load in moment_loads:
                load.wait()
            waited.add("moments")
        z_arrived(c, yh, 14)
        arrived(y_in.at[c], c, 18, y_far)

        low = (z_sum(c, yh) + wide(y_in, c))[:owned]
        for part_of in range(chunk // 128):
            lanes = slice(part_of * 128, (part_of + 1) * 128)
            here = pl.ds(c * (chunk // 128) + part_of, owned, stride=row_tiles)
            first_next, second_next, direction = adam_direction(low[:, lanes], first[here, :], second[here, :])
            first[here, :] = first_next
            second[here, :] = second_next
            dirs[c, yl, x, :owned, lanes] = direction

    def dirs_out(c):
        return dirs_hbm.at[:, :, :, pl.ds(c * chunk, chunk)]

    def out_copies(c):
        if DIR_X_FIRST[c]:
            return pltpu.make_async_copy(dirs.at[c, yl], dirs_out(c).at[yl], store_sem.at[c, 0])
        return pltpu.make_async_copy(dirs.at[c, :, x], dirs_out(c).at[:, x], store_sem.at[c, 0])

    barrier_done, projected_pairs, waited, gathered = [], set(), set(), set()

    def stage(s, c):
        if s == 0:
            if c // 2 not in projected_pairs:
                project(c // 2 * 2)
                projected_pairs.add(c // 2)
            if not barrier_done:
                pl.semaphore_wait(barrier, len(peers))
                barrier_done.append(True)
            reduce_first(c)
        elif s == 1:
            reduce_second(c)
        elif s == 2:
            reduce_last(c)
            gather_first(projected, projected.at[c], c, 4, AG_X_FIRST[c])
        elif s == 3:
            gather_second(projected, projected.at[c], c, 4, AG_X_FIRST[c])
        elif s == 4:
            gather_last(projected.at[c], c, 4, AG_X_FIRST[c])
            if "grads" not in waited:
                grads_load.wait()
                waited.add("grads")
            if c ^ 1 in gathered:
                gradient(c // 2 * 2)
            gathered.add(c)
        elif s == 5:
            done = sent[c][:-1]
            core_sum(c)
            for copy in done:
                copy.wait_send()
            del sent[c][: len(done)]
        elif s == 6:
            z_stage(c)
        elif s == 7:
            adam(c)
            gather_first(dirs, dirs_out(c), c, 19, DIR_X_FIRST[c])
        elif s == 8:
            done = sent[c][:8]
            gather_second(dirs, dirs_out(c), c, 19, DIR_X_FIRST[c])
            out_copies(c).start()
            for copy in done:
                copy.wait_send()
            del sent[c][: len(done)]
        else:
            gather_last(dirs_out(c), c, 19, DIR_X_FIRST[c])

    order, turns = [], [0] * CHUNKS
    for c in ORDER:
        order.append((None, c, turns[c]))
        turns[c] += 1
    moments = [
        pltpu.make_async_copy(first, first_out, store_sem.at[CHUNKS, 0]),
        pltpu.make_async_copy(second, second_out, store_sem.at[CHUNKS + 1, 0]),
    ]
    last_adam = [c for _, c, s in order if s == 7][-1]
    for _, c, s in order:
        stage(s, c)
        if s == 7 and c == last_adam:
            for copy in moments:
                copy.start()
    for c in range(CHUNKS):
        for copy in sent[c]:
            copy.wait_send()
    for c in range(CHUNKS):
        out_copies(c).wait()
    for copy in moments:
        copy.wait()


def exchange(activations, grads_t, projector, first, second, owned):
    features = activations.shape[1]
    width = grads_t.shape[1]
    depth, rank = projector.shape[1:]
    padded = -(-owned // 16) * 16
    chunk = rank // CHUNKS
    tokens = features // 8
    in_hbm = pl.BlockSpec(memory_space=pl.ANY)
    C = CHUNKS
    scratch = [
        pltpu.VMEM((features, depth), BF16),
        pltpu.VMEM((depth, rank), BF16),
        pltpu.VMEM((width, features), BF16),
        pltpu.VMEM(first.shape, F32),
        pltpu.VMEM(first.shape, F32),
        pltpu.VMEM((width + 16, 2 * chunk), F32),
        pltpu.VMEM((C, 2, 4, tokens, chunk), BF16),
        pltpu.VMEM((C, 6, tokens, chunk), BF16),
        pltpu.VMEM((C, 3, tokens, chunk), BF16),
        pltpu.VMEM((C, 3, tokens, chunk), BF16),
        pltpu.VMEM((C, 2, 4, tokens, chunk), BF16),
        pltpu.VMEM((C, 2, 2, 4, padded, chunk), BF16),
        pltpu.VMEM((C, 2, 4, padded, chunk), BF16),
        pltpu.VMEM((C, 3, 2, padded, chunk), BF16),
        pltpu.VMEM((C, 3, 2, padded, chunk), BF16),
        pltpu.VMEM((C, padded, chunk), BF16),
        pltpu.VMEM((C, padded, chunk), BF16),
        pltpu.VMEM((C, 2, 4, padded, chunk), BF16),
        pltpu.SemaphoreType.DMA((5 + C // 2,)),
        pltpu.SemaphoreType.DMA((C + 2, 2)),
        pltpu.SemaphoreType.DMA((C, 26)),
        pltpu.SemaphoreType.DMA((C, 26)),
    ]
    return pl.pallas_call(
        exchange_kernel,
        out_shape=(
            jax.ShapeDtypeStruct((2, 4, padded, rank), BF16),
            jax.ShapeDtypeStruct(first.shape, F32),
            jax.ShapeDtypeStruct(first.shape, F32),
        ),
        in_specs=[in_hbm] * 5,
        out_specs=(in_hbm,) * 3,
        scratch_shapes=scratch,
        compiler_params=pltpu.CompilerParams(
            collective_id=0, has_side_effects=True, vmem_limit_bytes=60 << 20
        ),
        name="exchange",
    )(activations, grads_t, projector, first, second)


EXPAND_ROWS = ((0, 48), (48, 80), (128, 48))
EXPAND_LANES = 512


def expand_kernel(
    dirs_hbm, basis_hbm, first_in, second_in, update_out, first_out, second_out,
    dirs, basis, update, first, second, load_sem, basis_sem, store_sem, sem,
):
    rank = dirs.shape[3]
    depth = basis.shape[0]
    owned = update.shape[1] // 8
    tiles = [pl.ds(lane, EXPAND_LANES) for lane in range(0, depth, EXPAND_LANES)]
    basis_loads = [
        pltpu.make_async_copy(basis_hbm.at[0, lanes], basis.at[lanes], basis_sem.at[index])
        for index, lanes in enumerate(tiles)
    ]
    loads = [
        pltpu.make_async_copy(dirs_hbm.at[:, :, pl.ds(*rows)], dirs.at[:, :, pl.ds(*rows)], load_sem.at[group])
        for group, rows in enumerate(EXPAND_ROWS)
    ]
    basis_loads[0].start()
    for load in loads[:1] + basis_loads[1:] + loads[1:]:
        load.start()
    moments_in = [
        pltpu.make_async_copy(first_in, first, sem.at[0]),
        pltpu.make_async_copy(second_in, second, sem.at[1]),
    ]
    moments_out = [
        pltpu.make_async_copy(first, first_out, sem.at[2]),
        pltpu.make_async_copy(second, second_out, sem.at[3]),
    ]
    for copy in moments_in:
        copy.start()
    stores = []
    for group, (start, rows) in enumerate(EXPAND_ROWS):
        loads[group].wait()
        kept = min(rows, owned - start)

        for index, lanes in enumerate(tiles):
            if group == 0:
                basis_loads[index].wait()
            total = lax.dot_general(
                dirs[:, :, pl.ds(start, rows), :].reshape(8 * rows, rank), basis[lanes, :],
                (((1,), (1,)), ((), ())), preferred_element_type=F32,
            )
            for part_of in range(EXPAND_LANES // 128):
                column = index * (EXPAND_LANES // 128) + part_of
                for yl in range(2):
                    for x in range(4):
                        at = (yl * 4 + x) * rows
                        update[column, pl.ds(start * 8 + x * 2 + yl, kept, stride=8), :] = total[
                            at : at + kept, part_of * 128 : (part_of + 1) * 128
                        ]
        for column in range(depth // 128):
            place = pl.ds(start * 8, kept * 8)
            store = pltpu.make_async_copy(
                update.at[column, place], update_out.at[place, pl.ds(column * 128, 128)], store_sem.at[group, column]
            )
            store.start()
            stores.append(store)
        if group == 0:
            for copy_in, copy_out in zip(moments_in, moments_out):
                copy_in.wait()
                copy_out.start()
    for store in stores + moments_out:
        store.wait()


def expand(dirs, projector, first, second, owned):
    depth, rank = projector.shape[1:]
    in_hbm = pl.BlockSpec(memory_space=pl.ANY)
    moment = jax.ShapeDtypeStruct(first.shape, F32)
    return pl.pallas_call(
        expand_kernel,
        out_shape=(jax.ShapeDtypeStruct((owned * 8, depth), F32), moment, moment),
        in_specs=[in_hbm] * 4,
        out_specs=(in_hbm,) * 3,
        scratch_shapes=[
            pltpu.VMEM(dirs.shape, BF16),
            pltpu.VMEM((depth, rank), BF16),
            pltpu.VMEM((depth // 128, owned * 8, 128), F32),
            pltpu.VMEM(first.shape, F32),
            pltpu.VMEM(first.shape, F32),
            pltpu.SemaphoreType.DMA((len(EXPAND_ROWS),)),
            pltpu.SemaphoreType.DMA((depth // EXPAND_LANES,)),
            pltpu.SemaphoreType.DMA((len(EXPAND_ROWS), depth // 128)),
            pltpu.SemaphoreType.DMA((4,)),
        ],
        compiler_params=pltpu.CompilerParams(vmem_limit_bytes=60 << 20),
        name="expand",
    )(dirs, projector, first, second)


def local(activations, out_grads, projector, first_moment, second_moment):
    owned, rank = first_moment.shape[1:]
    flat = (owned * (rank // 128), 128)
    dirs, first, second = exchange(
        activations, jnp.swapaxes(out_grads, 1, 2), projector, first_moment.reshape(flat), second_moment.reshape(flat),
        owned,
    )
    update, first, second = expand(dirs, projector, first, second, owned)
    update = update.reshape(owned, 8, -1).transpose(1, 0, 2)[None]
    return update, first.reshape(first_moment.shape), second.reshape(second_moment.shape)


def solution(mesh):
    in_specs = (
        P(None, "dp", "fsdp"),
        P(None, "dp", "fsdp"),
        P(None, "fsdp", None),
        P(None, ("fsdp", "dp"), None),
        P(None, ("fsdp", "dp"), None),
    )
    out_specs = (
        P(None, None, "dp", "fsdp"),
        P(None, ("fsdp", "dp"), None),
        P(None, ("fsdp", "dp"), None),
    )
    return jax.shard_map(local, mesh=mesh, in_specs=in_specs, out_specs=out_specs, check_vma=False)
```

time: 92.8 us -> 86.2 us (0.929)
  Pallas kernels: 92.1 us -> 85.4 us
    pallas_call x1, Pallas kernels: 83.1 us -> 77.9 us  [exchange(): pl.pallas_call(exchange_kernel, out_shape=(jax.ShapeDtypeStruct((2, 4, pa...]
    pallas_call x1, Pallas kernels: 9.03 us -> 7.55 us  [expand(): pl.pallas_call(expand_kernel, out_shape=(jax.ShapeDtypeStruct((owned * 8,...]
where the time goes in v3:
time: 86.2 us; the launch traced here: 86.1 us
  Pallas kernels  85.4 us (99%)
    pallas_call x1, Pallas kernels, exchange(): pl.pallas_call(exchange_kernel, out_shape=(jax.ShapeDtypeStruct((2, 4, pa...  77.9 us
    pallas_call x1, Pallas kernels, expand(): pl.pallas_call(expand_kernel, out_shape=(jax.ShapeDtypeStruct((owned * 8,...  7.55 us

profile of v3, /device:TPU:0, one launch (start us, length us, event | category | flops | bytes accessed | tf_op | source)
XLA Modules:
  0.0 86.1 jit_solution(6053250012174746094)
XLA Ops:
  0.6 77.9 %exchange.1 = (bf16[2,4,176,1024]{3,2,1,0:T(8,128)(2,1)}, f32[1376,128]{1,0:T(8,128)}, f32[1376,128]{1,0:T(8,128)}) custom-call(bf16[1,1024,1024]{2,1,0:T(8,128)(2,1)} %act_hbm.1, bf16[1,2752,1024]{2,1,0:T(8,128)(2,1)} %bitcast.10, bf16[1,1024,1024]{2,1,0:T(8,128)(2,1)} %basis_hbm.3, f32[1376,128]{1,0:T(8,128)} %bitcast.11, f32[1376,128]{1,0:T(8,128)} %bitcast.12), custom_call_target="tpu_custom_call" | custom-call | tf_op jit(solution)/shard_map/exchange/pallas_call | solution.py:371
  78.5 7.5 %expand.1 = (f32[1376,1024]{1,0:T(8,128)}, f32[1376,128]{1,0:T(8,128)}, f32[1376,128]{1,0:T(8,128)}) custom-call(bf16[2,4,176,1024]{3,2,1,0:T(8,128)(2,1)} %get-tuple-element.9.dirs_hbm, bf16[1,1024,1024]{2,1,0:T(8,128)(2,1)} %basis_hbm.3, f32[1376,128]{1,0:T(8,128)} %get-tuple-element.10.first_in, f32[1376,128]{1,0:T(8,128)} %get-tuple-element.11.second_in), custom_call_target="tpu_custom_call" | custom-call | tf_op jit(solution)/shard_map/expand/pallas_call | solution.py:460

commit v4 on v3

--- a/solution.py
+++ b/solution.py
@@ -203,19 +203,23 @@
 
         lax.fori_loop(0, 4, one, 0)
 
-        def two(pair, carry):
-            for which in range(2):
-                shift = which * owned % 8
-                start = pl.multiple_of(pair * (2 * owned) + which * owned - shift, 8)
+        def blocks_of(which):
+            shift = which * owned % 8
+
+            def two(block, carry):
+                start = pl.multiple_of(block * (2 * owned) + which * owned - shift, 8)
                 value = product[pl.ds(start, padded + 8), :]
                 value = value[shift : shift + padded].astype(BF16)
                 for k in range(2):
-                    terms[first_c + k, which, pair // 4, pair % 4] = value[:, k * chunk : (k + 1) * chunk]
-            return carry
-
-        lax.fori_loop(0, 8, two, 0)
+                    terms[first_c + k, which, block // 4, block % 4] = value[:, k * chunk : (k + 1) * chunk]
+                return carry
+
+            lax.fori_loop(0, 8, two, 0)
+
+        lax.cond(core == 0, lambda: blocks_of(1), lambda: blocks_of(0))
         for c in (first_c, first_c + 1):
             send(terms.at[c, 1 - core], core_in.at[c], c, 11, sibling)
+        lax.cond(core == 0, lambda: blocks_of(0), lambda: blocks_of(1))
 
     def core_sum(c):
         arrived(core_in.at[c], c, 11, sibling)
@@ -311,6 +315,9 @@
             del sent[c][: len(done)]
         else:
             gather_last(dirs_out(c), c, 19, DIR_X_FIRST[c])
+            for copy in sent[c]:
+                copy.wait_send()
+            out_copies(c).wait()
 
     order, turns = [], [0] * CHUNKS
     for c in ORDER:
@@ -326,11 +333,6 @@
         if s == 7 and c == last_adam:
             for copy in moments:
                 copy.start()
-    for c in range(CHUNKS):
-        for copy in sent[c]:
-            copy.wait_send()
-    for c in range(CHUNKS):
-        out_copies(c).wait()
     for copy in moments:
         copy.wait()
 
@@ -385,7 +387,7 @@
     )(activations, grads_t, projector, first, second)
 
 
-EXPAND_ROWS = ((0, 48), (48, 80), (128, 48))
+EXPAND_ROWS = ((0, 64), (64, 80), (144, 32))
 EXPAND_LANES = 512
 
 

time: 86.2 us -> 86.1 us (level)
  no operation moved by 1% of the time
where the time goes in v4:
time: 86.1 us; the launch traced here: 86 us
  Pallas kernels  85.2 us (99%)
    pallas_call x1, Pallas kernels, exchange(): pl.pallas_call(exchange_kernel, out_shape=(jax.ShapeDtypeStruct((2, 4, pa...  77.9 us
    pallas_call x1, Pallas kernels, expand(): pl.pallas_call(expand_kernel, out_shape=(jax.ShapeDtypeStruct((owned * 8,...  7.31 us

profile of v4, /device:TPU:0, one launch (start us, length us, event | category | flops | bytes accessed | tf_op | source)
XLA Modules:
  0.0 86.0 jit_solution(5193280887393163556)
XLA Ops:
  0.6 77.9 %exchange.1 = (bf16[2,4,176,1024]{3,2,1,0:T(8,128)(2,1)}, f32[1376,128]{1,0:T(8,128)}, f32[1376,128]{1,0:T(8,128)}) custom-call(bf16[1,1024,1024]{2,1,0:T(8,128)(2,1)} %act_hbm.1, bf16[1,2752,1024]{2,1,0:T(8,128)(2,1)} %bitcast.10, bf16[1,1024,1024]{2,1,0:T(8,128)(2,1)} %basis_hbm.3, f32[1376,128]{1,0:T(8,128)} %bitcast.11, f32[1376,128]{1,0:T(8,128)} %bitcast.12), custom_call_target="tpu_custom_call" | custom-call | tf_op jit(solution)/shard_map/exchange/pallas_call | solution.py:373
  78.5 7.3 %expand.1 = (f32[1376,1024]{1,0:T(8,128)}, f32[1376,128]{1,0:T(8,128)}, f32[1376,128]{1,0:T(8,128)}) custom-call(bf16[2,4,176,1024]{3,2,1,0:T(8,128)(2,1)} %get-tuple-element.9.dirs_hbm, bf16[1,1024,1024]{2,1,0:T(8,128)(2,1)} %basis_hbm.3, f32[1376,128]{1,0:T(8,128)} %get-tuple-element.10.first_in, f32[1376,128]{1,0:T(8,128)} %get-tuple-element.11.second_in), custom_call_target="tpu_custom_call" | custom-call | tf_op jit(solution)/shard_map/expand/pallas_call | solution.py:462

commit v5 on v4

--- a/solution.py
+++ b/solution.py
@@ -53,7 +53,8 @@
     x, yl = fs // 2, fs % 2
     chunk = basis.shape[1] // CHUNKS
     row_tiles = basis.shape[1] // 128
-    owned = first.shape[0] // row_tiles
+    flat = pl.ds(0, first_hbm.shape[0])
+    owned = first_hbm.shape[0] // row_tiles
     padded = dirs.shape[3]
     tokens = part.shape[3]
     features = act.shape[0]
@@ -80,8 +81,8 @@
     ]
     grads_load = pltpu.make_async_copy(grads_hbm.at[0], grads_t, load_sem.at[2 + CHUNKS // 2])
     moment_loads = [
-        pltpu.make_async_copy(first_hbm, first, load_sem.at[3 + CHUNKS // 2]),
-        pltpu.make_async_copy(second_hbm, second, load_sem.at[4 + CHUNKS // 2]),
+        pltpu.make_async_copy(first_hbm, first.at[flat], load_sem.at[3 + CHUNKS // 2]),
+        pltpu.make_async_copy(second_hbm, second.at[flat], load_sem.at[4 + CHUNKS // 2]),
     ]
     pairs = list(dict.fromkeys(c // 2 for c in ORDER))
     basis_loads[pairs[0]].start()
@@ -324,8 +325,8 @@
         order.append((None, c, turns[c]))
         turns[c] += 1
     moments = [
-        pltpu.make_async_copy(first, first_out, store_sem.at[CHUNKS, 0]),
-        pltpu.make_async_copy(second, second_out, store_sem.at[CHUNKS + 1, 0]),
+        pltpu.make_async_copy(first.at[flat], first_out, store_sem.at[CHUNKS, 0]),
+        pltpu.make_async_copy(second.at[flat], second_out, store_sem.at[CHUNKS + 1, 0]),
     ]
     last_adam = [c for _, c, s in order if s == 7][-1]
     for _, c, s in order:
@@ -350,8 +351,8 @@
         pltpu.VMEM((features, depth), BF16),
         pltpu.VMEM((depth, rank), BF16),
         pltpu.VMEM((width, features), BF16),
-        pltpu.VMEM(first.shape, F32),
-        pltpu.VMEM(first.shape, F32),
+        pltpu.VMEM((padded * (rank // 128), 128), F32),
+        pltpu.VMEM((padded * (rank // 128), 128), F32),
         pltpu.VMEM((width + 16, 2 * chunk), F32),
         pltpu.VMEM((C, 2, 4, tokens, chunk), BF16),
         pltpu.VMEM((C, 6, tokens, chunk), BF16),
@@ -397,7 +398,7 @@
 ):
     rank = dirs.shape[3]
     depth = basis.shape[0]
-    owned = update.shape[1] // 8
+    owned = update_out.shape[0] // 8
     tiles = [pl.ds(lane, EXPAND_LANES) for lane in range(0, depth, EXPAND_LANES)]
     basis_loads = [
         pltpu.make_async_copy(basis_hbm.at[0, lanes], basis.at[lanes], basis_sem.at[index])
@@ -467,7 +468,7 @@
         scratch_shapes=[
             pltpu.VMEM(dirs.shape, BF16),
             pltpu.VMEM((depth, rank), BF16),
-            pltpu.VMEM((depth // 128, owned * 8, 128), F32),
+            pltpu.VMEM((depth // 128, dirs.shape[2] * 8, 128), F32),
             pltpu.VMEM(first.shape, F32),
             pltpu.VMEM(first.shape, F32),
             pltpu.SemaphoreType.DMA((len(EXPAND_ROWS),)),

time: 86.1 us -> 86.1 us (level)
  no operation moved by 1% of the time
where the time goes in v5:
time: 86.1 us; the launch traced here: 86 us
  Pallas kernels  85.2 us (99%)
    pallas_call x1, Pallas kernels, exchange(): pl.pallas_call(exchange_kernel, out_shape=(jax.ShapeDtypeStruct((2, 4, pa...  77.9 us
    pallas_call x1, Pallas kernels, expand(): pl.pallas_call(expand_kernel, out_shape=(jax.ShapeDtypeStruct((owned * 8,...  7.33 us

profile of v5, /device:TPU:0, one launch (start us, length us, event | category | flops | bytes accessed | tf_op | source)
XLA Modules:
  0.0 86.0 jit_solution(11892891607144656519)
XLA Ops:
  0.6 77.9 %exchange.1 = (bf16[2,4,176,1024]{3,2,1,0:T(8,128)(2,1)}, f32[1376,128]{1,0:T(8,128)}, f32[1376,128]{1,0:T(8,128)}) custom-call(bf16[1,1024,1024]{2,1,0:T(8,128)(2,1)} %act_hbm.1, bf16[1,2752,1024]{2,1,0:T(8,128)(2,1)} %bitcast.10, bf16[1,1024,1024]{2,1,0:T(8,128)(2,1)} %basis_hbm.3, f32[1376,128]{1,0:T(8,128)} %bitcast.11, f32[1376,128]{1,0:T(8,128)} %bitcast.12), custom_call_target="tpu_custom_call" | custom-call | tf_op jit(solution)/shard_map/exchange/pallas_call | solution.py:374
  78.5 7.3 %expand.1 = (f32[1376,1024]{1,0:T(8,128)}, f32[1376,128]{1,0:T(8,128)}, f32[1376,128]{1,0:T(8,128)}) custom-call(bf16[2,4,176,1024]{3,2,1,0:T(8,128)(2,1)} %get-tuple-element.9.dirs_hbm, bf16[1,1024,1024]{2,1,0:T(8,128)(2,1)} %basis_hbm.3, f32[1376,128]{1,0:T(8,128)} %get-tuple-element.10.first_in, f32[1376,128]{1,0:T(8,128)} %get-tuple-element.11.second_in), custom_call_target="tpu_custom_call" | custom-call | tf_op jit(solution)/shard_map/expand/pallas_call | solution.py:463
